TPU v7x, 32 devices: a whole 2x2x4 slice. The times are simulated.
32 devices in a mesh: lon: 8 (over z, core), lat: 4 (over y, x).
Axes of the slice: x: 2, y: 2, z: 4, core: 2. Of those that a mesh axis runs over, the one named last changes fastest.
Arguments:
- latent: bfloat16 [96, 192, 512], P('lat', 'lon'), may hold values from -24 to 24
- ln1_gain: float32 [512], replicated, may hold values from 0.1 to 1.9
- qkv_weight: bfloat16 [512, 1536], replicated, may hold values from -0.25 to 0.25
- qkv_bias: float32 [1536], replicated, may hold values from -3 to 3
- bias_table: float32 [253, 8], replicated, may hold values from -4 to 242
- bias_index: int32 [72, 72], replicated, may hold values from 0 to 252
- proj_weight: bfloat16 [512, 512], replicated, may hold values from -0.25 to 0.25
- ln2_gain: float32 [512], replicated, may hold values from 0.1 to 1.9
- fc1_weight: bfloat16 [512, 2048], replicated, may hold values from -0.25 to 0.25
- fc1_bias: float32 [2048], replicated, may hold values from -3 to 3
- fc2_weight: bfloat16 [2048, 512], replicated, may hold values from -0.125 to 0.125
- merge_gain: float32 [2048], replicated, may hold values from 0.1 to 1.9
- reduce_weight: bfloat16 [2048, 1024], replicated, may hold values from -0.125 to 0.125
Outputs:
- coarse: bfloat16 [48, 96, 1024], P('lat', 'lon')
All inputs are finite; a program needn't handle non-finite values.
Results may differ from a plain program's by a relative error of at most 0.017.
Values may be sent and summed in bfloat16 or wider, within the bound.
A program may use at most 64 MiB of HBM per device.

v0:
```python
import jax
import jax.numpy as jnp
from jax import lax
from jax.sharding import PartitionSpec as P

WH = 6
WW = 12
SH = 3
SW = 6


EPSILON = 1e-05
MASKED = -1e30


def shifted_2(shard, axis, by):
    length = lax.axis_size(axis)
    return lax.ppermute(shard, axis, [(i, (i + by) % length) for i in range(length)])


def layer_norm(values, gain):
    values = values.astype(jnp.float32)
    center = values - jnp.mean(values, axis=-1, keepdims=True)
    spread = jnp.mean(center * center, axis=-1, keepdims=True)
    return center * lax.rsqrt(spread + EPSILON) * gain


def to_windows(tile, depth):
    tile_rows, tile_cols, channels = tile.shape
    blocks = tile.reshape(tile_rows // depth, depth, tile_cols // WW, WW, channels)
    return blocks.transpose(0, 2, 1, 3, 4).reshape(-1, depth * WW, channels)


def from_windows(windows, tile_rows, tile_cols, depth):
    channels = windows.shape[-1]
    blocks = windows.reshape(tile_rows // depth, tile_cols // WW, depth, WW, channels)
    return blocks.transpose(0, 2, 1, 3, 4).reshape(tile_rows, tile_cols, channels)


def window_attention(qkv_windows, bias, allowed, head_count):
    window_count, window_tokens, triple = qkv_windows.shape
    model_dim = triple // 3
    head_size = model_dim // head_count
    pieces = qkv_windows.reshape(window_count, window_tokens, 3, head_count, head_size)
    scores = jnp.einsum(
        "wqhc,wkhc->whqk", pieces[:, :, 0], pieces[:, :, 1], preferred_element_type=jnp.float32
    )
    scores = scores * head_size ** (-0.5) + bias
    scores = jnp.where(allowed, scores, MASKED)
    weights = jax.nn.softmax(scores, axis=-1).astype(jnp.bfloat16)
    mixed = jnp.einsum(
        "whqk,wkhc->wqhc", weights, pieces[:, :, 2], preferred_element_type=jnp.float32
    )
    return mixed.reshape(window_count, window_tokens, model_dim).astype(jnp.bfloat16)


def per_device(
    latent,
    ln1_gain,
    qkv_weight,
    qkv_bias,
    bias_table,
    bias_index,
    proj_weight,
    ln2_gain,
    fc1_weight,
    fc1_bias,
    fc2_weight,
    merge_gain,
    reduce_weight,
):
    tile_rows, tile_cols, model_dim = latent.shape
    head_count = bias_table.shape[1]
    window_tokens = WH * WW
    grid_rows = tile_rows * lax.axis_size("lat")
    lookup = (bias_index[:, :, None] == jnp.arange(bias_table.shape[0], dtype=jnp.int32)).astype(
        jnp.float32
    )
    table = jnp.einsum("qkn,nh->hqk", lookup, bias_table, precision=lax.Precision.HIGHEST)
    normed = layer_norm(latent, ln1_gain).astype(jnp.bfloat16)
    incoming = shifted_2(normed[:, :SW], "lon", -1)
    moved = jnp.concatenate([normed[:, SW:], incoming], axis=1)
    below = shifted_2(moved[:SH], "lat", -1)
    shifted = jnp.concatenate([moved[SH:], below], axis=0)
    flat = shifted.reshape(-1, model_dim)
    result = jnp.dot(flat, qkv_weight, preferred_element_type=jnp.float32) + qkv_bias
    qkv_tile = result.astype(jnp.bfloat16).reshape(shifted.shape[:-1] + (3 * model_dim,))
    band_rows = lax.axis_index("lat") * tile_rows + jnp.arange(tile_rows, dtype=jnp.int32)
    region = band_rows >= grid_rows - SH
    count_rows = band_rows.shape[0]
    window_region = jnp.broadcast_to(
        region.reshape(count_rows // WH, 1, WH, 1), (count_rows // WH, tile_cols // WW, WH, WW)
    )
    window_region = window_region.reshape(-1, window_tokens)
    allowed = (window_region[:, :, None] == window_region[:, None, :])[:, None]
    mixed = window_attention(to_windows(qkv_tile, WH), table, allowed, head_count)
    flat = mixed.reshape(-1, model_dim)
    attended = from_windows(
        jnp.dot(flat, proj_weight, preferred_element_type=jnp.float32)
        .astype(jnp.bfloat16)
        .reshape(mixed.shape),
        tile_rows,
        tile_cols,
        WH,
    )
    above = shifted_2(attended[tile_rows - SH :], "lat", 1)
    unshifted = jnp.concatenate([above, attended[: tile_rows - SH]], axis=0)
    leftmost = shifted_2(unshifted[:, tile_cols - SW :], "lon", 1)
    attention_out = jnp.concatenate([leftmost, unshifted[:, : tile_cols - SW]], axis=1)
    hidden = latent.astype(jnp.float32) + attention_out.astype(jnp.float32)
    normed_two = layer_norm(hidden, ln2_gain).astype(jnp.bfloat16).reshape(-1, model_dim)
    inner = jax.nn.gelu(
        jnp.dot(normed_two, fc1_weight, preferred_element_type=jnp.float32) + fc1_bias,
        approximate=False,
    ).astype(jnp.bfloat16)
    block = (
        hidden.reshape(-1, model_dim)
        + jnp.dot(inner, fc2_weight, preferred_element_type=jnp.float32)
    ).astype(jnp.bfloat16)
    quads = block.reshape(tile_rows // 2, 2, tile_cols // 2, 2, model_dim).transpose(0, 2, 3, 1, 4)
    quads = quads.reshape(tile_rows // 2, tile_cols // 2, 4 * model_dim)
    merged = layer_norm(quads, merge_gain).astype(jnp.bfloat16)
    result = jnp.dot(
        merged.reshape(-1, 4 * model_dim), reduce_weight, preferred_element_type=jnp.float32
    )
    return result.astype(jnp.bfloat16).reshape(tile_rows // 2, tile_cols // 2, 2 * model_dim)


def solution(mesh):
    in_specs = (P("lat", "lon", None), P(), P(), P(), P(), P(), P(), P(), P(), P(), P(), P(), P())
    out_specs = P("lat", "lon", None)
    return jax.shard_map(
        per_device, mesh=mesh, in_specs=in_specs, out_specs=out_specs, check_vma=False
    )
```

profile of v0, /device:TPU:0, one launch (start us, length us, event | category | flops | bytes accessed | tf_op | source)
XLA Modules:
  0.0 106.5 jit_solution(16243420334066673276)
XLA Ops:
  4.1 4.5 %collective-permute-start = (bf16[24,6,512]{2,1,0:T(8,128)(2,1)S(1)}, bf16[24,6,512]{2,1,0:T(8,128)(2,1)S(1)}, u32[]{:S(2)}, u32[]{:S(2)}) collective-permute-start(bf16[24,6,512]{2,1,0:T(8,128)(2,1)S(1)} %slice.45), channel_id=1, source_target_pairs={{0,28},{4,0},{8,4},{12,8},{16,12},{20,16},{24,20},{28,24},{1,29},{... | collective-permute-start | bytes 442376 | tf_op jit(solution)/shard_map/ppermute | solution.py:18
  8.9 3.7 %fusion.26 = f32[8,72,72]{2,0,1:T(8,128)S(1)} fusion(s32[72,72]{1,0:T(8,128)S(1)} %copy-done.5, f32[253,8]{0,1:T(8,128)S(1)} %copy-done.6), kind=kOutput, calls=%fused_computation.52 | convolution fusion | flops 127220544 | bytes 194720 | tf_op jit(solution)/shard_map/qkn,nh->hqk/dot_general | solution.py:79
  13.9 2.5 %collective-permute-start.1 = (bf16[3,24,512]{2,1,0:T(8,128)(2,1)S(1)}, bf16[3,24,512]{2,1,0:T(8,128)(2,1)S(1)}, u32[]{:S(2)}, u32[]{:S(2)}) collective-permute-start(bf16[3,24,512]{2,1,0:T(8,128)(2,1)S(1)} %pad_maximum_fusion.3), channel_id=1, source_target_pairs={{0,3},{1,0},{2,1},{3,2},{4,7},{5,4},{6,5},{7,6},{8,11},{9,8},{10,9... | collective-permute-start | bytes 221192 | tf_op jit(solution)/shard_map/ppermute | solution.py:18
  16.5 1.9 %collective-permute-done.1 = bf16[3,24,512]{2,1,0:T(8,128)(2,1)S(1)} collective-permute-done((bf16[3,24,512]{2,1,0:T(8,128)(2,1)S(1)}, bf16[3,24,512]{2,1,0:T(8,128)(2,1)S(1)}, u32[]{:S(2)}, u32[]{:S(2)}) %collective-permute-start.1) | collective-permute-done | bytes 73760 | tf_op jit(solution)/shard_map/ppermute | solution.py:18
  18.5 2.3 %add_convert_fusion = bf16[576,1536]{1,0:T(8,128)(2,1)} fusion(bf16[576,512]{1,0:T(8,128)(2,1)S(1)} %bitcast.66, bf16[512,1536]{1,0:T(8,128)(2,1)S(1)} %copy-done.4, f32[1536]{0:T(1024)S(1)} %copy-done.7), kind=kOutput, calls=%fused_computation.22 | convolution fusion | flops 907739136 | bytes 3938304 | tf_op jit(solution)/shard_map/dot_general | solution.py:86
  20.7 3.8 %reshape_reshape.9 = bf16[4,6,2,12,1536]{4,3,2,1,0:T(8,128)(2,1)} reshape(bf16[576,1536]{1,0:T(8,128)(2,1)} %add_convert_fusion) | data formatting | bytes 3538944 | tf_op jit(solution)/shard_map/reshape;reshape | solution.py:30
  24.5 4.7 %copy.17 = bf16[4,2,6,12,1536]{4,1,0,3,2:T(2,128)(2,1)} copy(bf16[4,2,6,12,1536]{4,3,1,2,0:T(8,128)(2,1)} %bitcast.63) | data formatting | bytes 3538944 | tf_op jit(solution)/shard_map/transpose | solution.py:31
  29.2 6.8 %reshape_reshape.10 = bf16[8,72,3,8,64]{4,3,2,0,1:T(8,128)(2,1)} reshape(bf16[4,2,6,12,1536]{4,1,0,3,2:T(2,128)(2,1)} %copy.17) | data formatting | bytes 3538944 | tf_op jit(solution)/shard_map/reshape;reshape | solution.py:44
  36.0 4.6 %fusion.84 = (bf16[8,72,1,8,64]{4,3,2,0,1:T(8,128)(2,1)S(1)}, bf16[8,72,1,8,64]{4,3,2,0,1:T(8,128)(2,1)}, bf16[8,72,1,8,64]{4,3,2,0,1:T(8,128)(2,1)}) fusion(bf16[8,72,3,8,64]{4,3,2,0,1:T(8,128)(2,1)} %reshape_reshape.10), kind=kLoop, calls=%fused_computation.112 | loop fusion | bytes 3538944 | tf_op jit(solution)/shard_map/slice | solution.py:52
  40.6 3.1 %copy.28 = bf16[8,72,1,8,64]{1,4,3,0,2:T(8,128)(2,1)} copy(bf16[8,72,1,8,64]{4,3,2,0,1:T(8,128)(2,1)} %get-tuple-element.8) | data formatting | bytes 1179648
  43.7 3.1 %copy.29 = bf16[8,72,1,8,64]{1,4,3,0,2:T(8,128)(2,1)} copy(bf16[8,72,1,8,64]{4,3,2,0,1:T(8,128)(2,1)} %get-tuple-element.9) | data formatting | bytes 1179648
  46.7 2.1 %copy.27 = bf16[8,72,1,8,64]{1,4,3,0,2:T(8,128)(2,1)} copy(bf16[8,72,1,8,64]{4,3,2,0,1:T(8,128)(2,1)S(1)} %get-tuple-element.7) | data formatting | bytes 1179648
  48.8 4.4 %fusion.85 = (f32[8,8,72]{2,1,0:T(8,128)S(1)}, f32[8,8,72,72]{2,3,1,0:T(8,128)}) fusion(f32[8,72,72]{1,2,0:T(8,128)} %copy.21, pred[8,72,72]{1,2,0:T(8,128)(4,1)S(1)} %broadcast_compare_fusion, bf16[8,72,1,8,64]{1,4,3,0,2:T(8,128)(2,1)} %copy.29, bf16[8,72,1,8,64]{1,4,3,0,2:T(8,128)(2,1)} %copy.28), kind=kOutput, calls=%fused_computation.113 | convolution fusion | flops 44126280 | bytes 2732544 | tf_op jit(solution)/shard_map/sub | solution.py:50
  53.2 2.1 %fusion.17 = bf16[8,72,8,64]{1,3,2,0:T(8,128)(2,1)S(1)} fusion(f32[8,8,72,72]{2,3,1,0:T(8,128)} %get-tuple-element.11, f32[8,8,72]{2,1,0:T(8,128)S(1)} %get-tuple-element.10, bf16[8,72,1,8,64]{1,4,3,0,2:T(8,128)(2,1)S(1)} %copy-done.1), kind=kOutput, calls=%fused_computation.35 | convolution fusion | flops 43425792 | bytes 2525184 | tf_op jit(solution)/shard_map/whqk,wkhc->wqhc/dot_general | solution.py:51
  57.7 1.7 %convolution_convert_fusion.1 = bf16[576,512]{1,0:T(8,128)(2,1)S(1)} fusion(bf16[576,512]{0,1:T(8,128)(2,1)} %convert_element_type.71, bf16[512,512]{1,0:T(8,128)(2,1)} %param.19), kind=kOutput, calls=%fused_computation.36 | convolution fusion | flops 302284800 | bytes 1703936 | tf_op jit(solution)/shard_map/dot_general | solution.py:99
  61.8 2.4 %collective-permute-start.2 = (bf16[3,24,512]{2,1,0:T(8,128)(2,1)S(1)}, bf16[3,24,512]{2,1,0:T(8,128)(2,1)S(1)}, u32[]{:S(2)}, u32[]{:S(2)}) collective-permute-start(bf16[3,24,512]{2,1,0:T(8,128)(2,1)S(1)} %slice.51), channel_id=1, source_target_pairs={{0,1},{1,2},{2,3},{3,0},{4,5},{5,6},{6,7},{7,4},{8,9},{9,10},{10,1... | collective-permute-start | bytes 221192 | tf_op jit(solution)/shard_map/ppermute | solution.py:18
  64.2 3.2 %collective-permute-done.2 = bf16[3,24,512]{2,1,0:T(8,128)(2,1)S(1)} collective-permute-done((bf16[3,24,512]{2,1,0:T(8,128)(2,1)S(1)}, bf16[3,24,512]{2,1,0:T(8,128)(2,1)S(1)}, u32[]{:S(2)}, u32[]{:S(2)}) %collective-permute-start.2) | collective-permute-done | bytes 73760 | tf_op jit(solution)/shard_map/ppermute | solution.py:18
  67.8 6.9 %collective-permute-done.3 = bf16[24,6,512]{2,1,0:T(8,128)(2,1)S(1)} collective-permute-done((bf16[24,6,512]{2,1,0:T(8,128)(2,1)S(1)}, bf16[24,6,512]{2,1,0:T(8,128)(2,1)S(1)}, u32[]{:S(2)}, u32[]{:S(2)}) %collective-permute-start.3) | collective-permute-done | bytes 147488 | tf_op jit(solution)/shard_map/ppermute | solution.py:18
  77.5 14.7 %fusion.31 = f32[576,512]{1,0:T(8,128)} fusion(f32[24,24,512]{2,1,0:T(8,128)S(1)} %get-tuple-element.6, bf16[2048,512]{1,0:T(8,128)(2,1)S(1)} %copy-done, bf16[576,512]{1,0:T(8,128)(2,1)} %bitcast.67, bf16[512,2048]{1,0:T(8,128)(2,1)} %param.21, f32[2048]{0:T(1024)S(1)} %copy-done.8), kind=kOutput, calls=%fused_computation.57 | convolution fusion | flops 2494660608 | bytes 7151616 | tf_op jit(solution)/shard_map/dot_general | solution.py:118
  92.2 2.0 %reshape.107 = f32[12,2,12,2,512]{4,3,2,1,0:T(2,128)S(1)} reshape(f32[576,512]{1,0:T(8,128)} %fusion.31) | data formatting | bytes 2359296 | tf_op jit(solution)/shard_map/convert_element_type | solution.py:22
  95.3 1.9 %copy.35 = f32[12,2,12,2,512]{4,1,3,2,0:T(2,128)} copy(f32[12,2,12,2,512]{4,3,2,1,0:T(2,128)S(1)} %reshape.107) | data formatting | bytes 2359296 | tf_op jit(solution)/shard_map/convert_element_type | solution.py:22
  98.7 2.3 %reshape.105 = f32[144,2048]{1,0:T(8,128)S(1)} reshape(f32[12,12,2,2,512]{4,3,2,1,0:T(2,128)} %bitcast.64) | data formatting | bytes 2359296 | tf_op jit(solution)/shard_map/convert_element_type | solution.py:22
  101.0 3.7 %convolution_convert_fusion.2 = bf16[144,1024]{1,0:T(8,128)(2,1)} fusion(bf16[2048,1024]{1,0:T(8,128)(2,1)} %param.25, f32[144,2048]{1,0:T(8,128)S(1)} %reshape.105, f32[2048]{0:T(1024)S(1)} %copy-done.2, f32[144]{0:T(256)S(1)} %rsqrt.30, f32[144]{0:T(256)S(1)} %div.35), kind=kOutput, calls=%fused_computation.37 | convolution fusion | flops 605306880 | bytes 5678208 | tf_op jit(solution)/shard_map/dot_general | solution.py:123
  104.7 1.8 %reshape.104 = bf16[12,12,1024]{2,1,0:T(8,128)(2,1)} reshape(bf16[144,1024]{1,0:T(8,128)(2,1)} %convolution_convert_fusion.2) | data formatting | bytes 589824 | tf_op jit(solution)/shard_map/reshape | solution.py:126
  (54 shorter events, 16.0 us)
Async XLA Ops:
  0.0 77.5 %copy-start = (bf16[2048,512]{1,0:T(8,128)(2,1)S(1)}, bf16[2048,512]{1,0:T(8,128)(2,1)}, u32[]{:S(2)}) copy-start(bf16[2048,512]{1,0:T(8,128)(2,1)} %param.23) | copy-start | bytes 6291460
  0.0 8.8 %copy-start.6 = (f32[253,8]{0,1:T(8,128)S(1)}, f32[253,8]{0,1:T(8,128)}, u32[]{:S(2)}) copy-start(f32[253,8]{0,1:T(8,128)} %param.17) | copy-start | bytes 24292
  0.0 8.9 %copy-start.5 = (s32[72,72]{1,0:T(8,128)S(1)}, s32[72,72]{1,0:T(8,128)}, u32[]{:S(2)}) copy-start(s32[72,72]{1,0:T(8,128)} %param.18) | copy-start | bytes 62212
  4.1 9.7 %collective-permute-start = (bf16[24,6,512]{2,1,0:T(8,128)(2,1)S(1)}, bf16[24,6,512]{2,1,0:T(8,128)(2,1)S(1)}, u32[]{:S(2)}, u32[]{:S(2)}) collective-permute-start(bf16[24,6,512]{2,1,0:T(8,128)(2,1)S(1)} %slice.45), channel_id=1, source_target_pairs={{0,28},{4,0},{8,4},{12,8},{16,12},{20,16},{24,20},{28,24},{1,29},{... | collective-permute-start | bytes 442376 | tf_op jit(solution)/shard_map/ppermute | solution.py:18
  12.6 5.8 %copy-start.7 = (f32[1536]{0:T(1024)S(1)}, f32[1536]{0:T(1024)}, u32[]{:S(2)}) copy-start(f32[1536]{0:T(1024)} %param.16) | copy-start | bytes 18436
  13.7 4.7 %copy-start.4 = (bf16[512,1536]{1,0:T(8,128)(2,1)S(1)}, bf16[512,1536]{1,0:T(8,128)(2,1)}, u32[]{:S(2)}) copy-start(bf16[512,1536]{1,0:T(8,128)(2,1)} %param.15) | copy-start | bytes 4718596
  13.9 4.5 %collective-permute-start.1 = (bf16[3,24,512]{2,1,0:T(8,128)(2,1)S(1)}, bf16[3,24,512]{2,1,0:T(8,128)(2,1)S(1)}, u32[]{:S(2)}, u32[]{:S(2)}) collective-permute-start(bf16[3,24,512]{2,1,0:T(8,128)(2,1)S(1)} %pad_maximum_fusion.3), channel_id=1, source_target_pairs={{0,3},{1,0},{2,1},{3,2},{4,7},{5,4},{6,5},{7,6},{8,11},{9,8},{10,9... | collective-permute-start | bytes 221192 | tf_op jit(solution)/shard_map/ppermute | solution.py:18
  48.8 4.4 %copy-start.1 = (bf16[8,72,1,8,64]{1,4,3,0,2:T(8,128)(2,1)S(1)}, bf16[8,72,1,8,64]{1,4,3,0,2:T(8,128)(2,1)}, u32[]{:S(2)}) copy-start(bf16[8,72,1,8,64]{1,4,3,0,2:T(8,128)(2,1)} %copy.27) | copy-start | bytes 1769476
  61.8 5.7 %collective-permute-start.2 = (bf16[3,24,512]{2,1,0:T(8,128)(2,1)S(1)}, bf16[3,24,512]{2,1,0:T(8,128)(2,1)S(1)}, u32[]{:S(2)}, u32[]{:S(2)}) collective-permute-start(bf16[3,24,512]{2,1,0:T(8,128)(2,1)S(1)} %slice.51), channel_id=1, source_target_pairs={{0,1},{1,2},{2,3},{3,0},{4,5},{5,6},{6,7},{7,4},{8,9},{9,10},{10,1... | collective-permute-start | bytes 221192 | tf_op jit(solution)/shard_map/ppermute | solution.py:18
  64.2 12.2 %copy-start.3 = (f32[512]{0:T(512)S(1)}, f32[512]{0:T(512)}, u32[]{:S(2)}) copy-start(f32[512]{0:T(512)} %param.20) | copy-start | bytes 6148
  67.5 10.0 %copy-start.8 = (f32[2048]{0:T(1024)S(1)}, f32[2048]{0:T(1024)}, u32[]{:S(2)}) copy-start(f32[2048]{0:T(1024)} %param.22) | copy-start | bytes 24580
  67.5 7.1 %collective-permute-start.3 = (bf16[24,6,512]{2,1,0:T(8,128)(2,1)S(1)}, bf16[24,6,512]{2,1,0:T(8,128)(2,1)S(1)}, u32[]{:S(2)}, u32[]{:S(2)}) collective-permute-start(bf16[24,6,512]{2,1,0:T(8,128)(2,1)S(1)} %pad_maximum_fusion.2), channel_id=1, source_target_pairs={{0,4},{4,8},{8,12},{12,16},{16,20},{20,24},{24,28},{28,0},{1,5},{5... | collective-permute-start | bytes 442376 | tf_op jit(solution)/shard_map/ppermute | solution.py:18
  97.2 3.8 %copy-start.2 = (f32[2048]{0:T(1024)S(1)}, f32[2048]{0:T(1024)}, u32[]{:S(2)}) copy-start(f32[2048]{0:T(1024)} %param.24) | copy-start | bytes 24580
where the time goes:
time: 107 us
  local copies, waits for them, and re-layouts  42.2 us (39%)
  matrix products  32.7 us (31%)
  waiting for transfers between devices  12 us (11%)
  starting transfers between devices  9.65 us (9%)
  other arithmetic  9.63 us (9%)
    dot_general x1, matrix products, per_device(): jnp.dot(inner, fc2_weight, preferred_element_type=jnp.float32)  14.7 us
    ppermute x4, waiting for transfers between devices, shifted_2(): lax.ppermute(shard, axis, [(i, (i + by) % length) for i in range(length)])  12 us
    ppermute x4, starting transfers between devices, shifted_2(): lax.ppermute(shard, axis, [(i, (i + by) % length) for i in range(length)])  9.65 us
    unnamed x21, local copies, waits for them, and re-layouts  8.28 us
    another operation x1, local copies, waits for them, and re-layouts, window_attention(): qkv_windows.reshape(window_count, window_tokens, 3, head_count, head_size)  6.78 us
    convert_element_type x3, local copies, waits for them, and re-layouts, layer_norm(): values = values.astype(jnp.float32)  6.2 us
    transpose x1, local copies, waits for them, and re-layouts, to_windows(): return blocks.transpose(0, 2, 1, 3, 4).reshape(-1, depth * WW, channels)  4.71 us
    slice x1, local copies, waits for them, and re-layouts, window_attention(): pieces[:, :, 2]  4.56 us
  transfers between devices with their start and end apart: 4, of which 3 were waited for; matrix products, arithmetic and copies ran while one was open for 5% of the time, Pallas kernels for 0%

commit v1 on v0

v1 whole, which is shorter than its diff:
```python
import functools

import jax
import jax.numpy as jnp
import numpy as np
from jax import lax
from jax.experimental import pallas as pl
from jax.experimental.pallas import tpu as pltpu
from jax.sharding import PartitionSpec as P

WH = 6
WW = 12
SH = 3
SW = 6
WT = WH * WW
WP = 80

EPSILON = 1e-05
MASKED = -1e30
MESH = pl.DeviceIdType.MESH


def up16(n):
    return (n + 15) // 16 * 16


def one_hot(rows, cols, pairs):
    out = np.zeros((rows, cols), np.float32)
    for r, c in pairs:
        out[r, c] = 1.0
    return out.astype(jnp.bfloat16)


@functools.lru_cache(None)
def plan(tr, tc):
    nb, nc = tr // WH, tc // WW
    windows = [(b, c) for b in range(nb - 1) for c in range(nc - 1)]
    inner = len(windows)
    windows += [(b, nc - 1) for b in range(nb - 1)]
    windows += [(nb - 1, c) for c in range(nc)]
    slot = {}
    for w, (b, c) in enumerate(windows):
        for r in range(WH):
            for k in range(WW):
                slot[b * WH + r, c * WW + k] = w * WP + r * WW + k
    east = [(i, j) for i in range(SH, tr) for j in range(SW)]
    south = [(i, j) for i in range(SH) for j in range(SW, tc)]
    corner = [(i, j) for i in range(SH) for j in range(SW)]
    sizes = [up16(len(x)) for x in (east, south, corner)]
    starts = [0, sizes[0], sizes[0] + sizes[1]]
    halo = sum(sizes)
    packed = {}
    for s, x in zip(starts, (east, south, corner)):
        for n, cell in enumerate(x):
            packed[cell] = s + n
    own = tr * tc
    pack = one_hot(halo, own, [(v, i * tc + j) for (i, j), v in packed.items()])
    rows = len(windows) * WP
    p_lat, p_halo, back = [], [], []
    for (i, j), s in slot.items():
        gi, gj = i + SH, j + SW
        wi, wj = gi % tr, gj % tc
        if gi < tr and gj < tc:
            p_lat.append((s, gi * tc + gj))
        else:
            p_halo.append((s, packed[wi, wj]))
            back.append((packed[wi, wj], s - inner * WP))
    p_lat = one_hot(rows, own, p_lat)
    p_halo = one_hot(rows, halo, p_halo)[inner * WP:]
    back = one_hot(halo, rows - inner * WP, back)
    first_r, first_c = -(-SH // 2), -(-SW // 2)
    cells = [(a, b) for a in range(tr // 2) for b in range(tc // 2)]
    free = [x for x in cells if x[0] >= first_r and x[1] >= first_c]
    n1 = len(free) // 16 * 16
    order = free + [x for x in cells if x not in set(free)]
    n2 = len(order) - n1
    f_lat, f_att, f_ret = [], [], []
    for n, (a, b) in enumerate(order):
        for q in range(4):
            i, j = 2 * a + q % 2, 2 * b + q // 2
            t = q * n1 + n if n < n1 else 4 * n1 + q * n2 + n - n1
            f_lat.append((t, i * tc + j))
            if i >= SH and j >= SW:
                f_att.append((t, slot[i - SH, j - SW]))
            else:
                f_ret.append((t - 4 * n1, packed[i, j]))
    f_lat = one_hot(own, own, f_lat)
    f_att = one_hot(own, rows, f_att)
    f_ret = one_hot(4 * n2, halo, f_ret)
    wide = up16(tc // 2)
    out = one_hot(tr // 2 * wide, len(order), [(a * wide + b, n) for n, (a, b) in enumerate(order)])
    mats = dict(pack=pack, p_lat=p_lat, p_halo=p_halo, back=back, f_lat=f_lat, f_att=f_att, f_ret=f_ret, out=out)
    return mats, len(windows), inner, nc, sizes, starts, n1, n2, wide


def norm(values, gain):
    center = values - jnp.mean(values, axis=-1, keepdims=True)
    spread = jnp.mean(center * center, axis=-1, keepdims=True)
    return center * lax.rsqrt(spread + EPSILON) * gain


def dot(a, b):
    return jnp.dot(a, b, preferred_element_type=jnp.float32)


MATS = ("pack", "p_lat", "p_halo", "back", "f_lat", "f_att", "f_ret", "out")


def kernel(info, heads, lon_size, lat_size, *refs):
    (nw, inner, nc, sizes, starts, n1, n2, wide) = info
    (latent_h, g1, wqkv_h, bqkv, btab, bidx, wproj_h, g2, wfc1_h, bfc1, wfc2_h, gm, wred_h) = refs[:13]
    mats_h = refs[13:21]
    o_ref = refs[21]
    (lat, wqkv, wproj, wfc1, wfc2, wred) = refs[22:28]
    mats = dict(zip(MATS, refs[28:36]))
    (send1, recv1, send2, recv2, qkv, mixed, att, bias, last_bias, idx, tab, hid, inside, merged) = refs[36:50]
    (load_sem, s1, r1, s2, r2) = refs[50:55]
    m = dict(zip(MATS, range(7, 15)))
    dim = lat.shape[1]
    head = dim // heads
    group = 256 // head
    groups = heads // group

    me_lon, me_lat = lax.axis_index("lon"), lax.axis_index("lat")
    west, east = lax.rem(me_lon + lon_size - 1, lon_size), lax.rem(me_lon + 1, lon_size)
    north, south = lax.rem(me_lat + lat_size - 1, lat_size), lax.rem(me_lat + 1, lat_size)
    to1 = [(west, me_lat), (me_lon, north), (west, north)]
    to2 = [(east, me_lat), (me_lon, south), (east, south)]
    barrier = pltpu.get_barrier_semaphore()
    for lo, la in to1 + to2:
        pl.semaphore_signal(barrier, inc=1, device_id={"lon": lo, "lat": la}, device_id_type=MESH)

    loads = {}

    def load(name, src, dst, n):
        loads[name] = pltpu.make_async_copy(src, dst, load_sem.at[n])
        loads[name].start()

    load("lat", latent_h, lat, 0)
    hbm = dict(zip(MATS, mats_h))
    load("pack", hbm["pack"], mats["pack"], m["pack"])
    load("p_lat", hbm["p_lat"], mats["p_lat"], m["p_lat"])
    load("wqkv", wqkv_h, wqkv, 1)
    load("p_halo", hbm["p_halo"], mats["p_halo"], m["p_halo"])
    load("wproj", wproj_h, wproj, 2)
    for name in ("back", "f_lat", "f_att"):
        load(name, hbm[name], mats[name], m[name])
    load("wfc1", wfc1_h, wfc1, 3)
    load("wfc2", wfc2_h, wfc2, 4)
    for name in ("f_ret", "out"):
        load(name, hbm[name], mats[name], m[name])
    load("wred", wred_h, wred, 5)

    def copies(src, dst, ss, rs, to):
        return [
            pltpu.make_async_remote_copy(
                src_ref=src.at[pl.ds(starts[k], sizes[k])],
                dst_ref=dst.at[pl.ds(starts[k], sizes[k])],
                send_sem=ss.at[k],
                recv_sem=rs.at[k],
                device_id={"lon": to[k][0], "lat": to[k][1]},
                device_id_type=MESH,
            )
            for k in range(3)
        ]

    loads["lat"].wait()
    loads["pack"].wait()
    send1[...] = dot(mats["pack"][...], lat[...]).astype(jnp.bfloat16)
    pl.semaphore_wait(barrier, 6)
    first = copies(send1, recv1, s1, r1, to1)
    for c in first:
        c.start()

    tab[...] = jnp.zeros_like(tab)
    tab[0 : btab.shape[0], 0:heads] = btab[...]
    idx[...] = jnp.zeros_like(idx)
    idx[0:WT, 0:WT] = bidx[...]
    lines = tab[...].T
    where = idx[...]
    low, high = jnp.bitwise_and(where, 127), where >= 128
    lane = lax.broadcasted_iota(jnp.int32, (WP, 128), 1)
    row = lax.broadcasted_iota(jnp.int32, (WP, 128), 0)
    other = jnp.where((row >= SH * WW) != (lane >= SH * WW), MASKED, 0.0)
    other = jnp.where(me_lat == lat_size - 1, other, 0.0)
    for h in range(heads):
        a = jnp.broadcast_to(lines[h : h + 1, 0:128], (WP, 128))
        b = jnp.broadcast_to(lines[h : h + 1, 128:256], (WP, 128))
        a = jnp.take_along_axis(a, low, axis=1, mode="promise_in_bounds")
        b = jnp.take_along_axis(b, low, axis=1, mode="promise_in_bounds")
        value = jnp.where(lane < WT, jnp.where(high, b, a), MASKED)
        bias[h * WP : (h + 1) * WP, :] = value
        last_bias[h * WP : (h + 1) * WP, :] = value + other

    lanes = lax.broadcasted_iota(jnp.int32, (1, 256), 1)
    picks = [
        jnp.where((lanes >= k * head) & (lanes < (k + 1) * head), head**-0.5, 0.0).astype(jnp.bfloat16)
        for k in range(group)
    ]

    def project(at, rows, tokens):
        normed = norm(tokens, g1[...]).astype(jnp.bfloat16)
        qkv[at : at + rows, :] = (dot(normed, wqkv[...]) + bqkv[...]).astype(jnp.bfloat16)

    def attend(w, table):
        at = pl.multiple_of(w * WP, 16)
        for g in range(groups):
            col = g * 256
            q = qkv[pl.ds(at, WP), col : col + 256]
            k = qkv[pl.ds(at, 128), dim + col : dim + col + 256]
            v = qkv[pl.ds(at, 128), 2 * dim + col : 2 * dim + col + 256]
            stacked = jnp.concatenate([q * p for p in picks], axis=0)
            scores = lax.dot_general(
                stacked, k, (((1,), (1,)), ((), ())), preferred_element_type=jnp.float32
            )
            scores = scores + table[g * group * WP : (g + 1) * group * WP, :]
            e = jnp.exp(scores - jnp.max(scores, axis=-1, keepdims=True))
            weights = (e * (1.0 / jnp.sum(e, axis=-1, keepdims=True))).astype(jnp.bfloat16)
            full = dot(weights, v)
            total = full[0:WP]
            for n in range(1, group):
                total = jnp.where(lanes >= n * head, full[n * WP : (n + 1) * WP], total)
            mixed[pl.ds(at, WP), col : col + 256] = total.astype(jnp.bfloat16)

    def attend_range(lo, hi, table):
        def body(w, carry):
            attend(w, table)
            return carry

        lax.fori_loop(lo, hi, body, 0)

    cut, end = inner * WP, nw * WP
    loads["p_lat"].wait()
    loads["wqkv"].wait()
    qkv[cut : cut + 48, :] = jnp.zeros((48, 3 * dim), jnp.bfloat16)
    qkv[end : end + 48, :] = jnp.zeros((48, 3 * dim), jnp.bfloat16)
    project(0, cut, dot(mats["p_lat"][0:cut, :], lat[...]))
    attend_range(0, inner, bias)
    loads["wproj"].wait()
    att[0:cut, :] = dot(mixed[0:cut, :], wproj[...]).astype(jnp.bfloat16)

    loads["p_halo"].wait()
    for c in first:
        c.wait()
    project(cut, end - cut, dot(mats["p_lat"][cut:end, :], lat[...]) + dot(mats["p_halo"][...], recv1[...]))
    attend_range(inner, nw - nc, bias)
    attend_range(nw - nc, nw, last_bias)
    att[cut:end, :] = dot(mixed[cut:end, :], wproj[...]).astype(jnp.bfloat16)
    loads["back"].wait()
    send2[...] = dot(mats["back"][...], att[cut:end, :]).astype(jnp.bfloat16)
    second = copies(send2, recv2, s2, r2, to2)
    for c in second:
        c.start()

    loads["f_lat"].wait()
    loads["f_att"].wait()
    loads["wfc1"].wait()
    loads["wfc2"].wait()

    def feed(at, rows, hidden):
        normed = norm(hidden, g2[...]).astype(jnp.bfloat16)
        hid[0:rows, :] = hidden
        step = 512
        for c in range(0, wfc1.shape[1], step):
            x = dot(normed, wfc1[:, c : c + step]) + bfc1[:, c : c + step]
            x = 0.5 * x * (1.0 + lax.erf(x * 0.7071067811865476))
            inside[0:rows, c : c + step] = x.astype(jnp.bfloat16)
        block = (hid[0:rows, :] + dot(inside[0:rows, :], wfc2[...])).astype(jnp.bfloat16).astype(jnp.float32)
        n = rows // 4
        parts = [block[q * n : (q + 1) * n] for q in range(4)]
        mean = sum(jnp.sum(p, axis=-1, keepdims=True) for p in parts) * (1.0 / (4 * dim))
        parts = [p - mean for p in parts]
        spread = sum(jnp.sum(p * p, axis=-1, keepdims=True) for p in parts) * (1.0 / (4 * dim))
        inv = lax.rsqrt(spread + EPSILON)
        for q, p in enumerate(parts):
            cols = slice(q * dim, (q + 1) * dim)
            merged[at : at + n, cols] = (p * inv * gm[:, cols]).astype(jnp.bfloat16)

    mid = 4 * n1
    feed(0, mid, dot(mats["f_lat"][0:mid, :], lat[...]) + dot(mats["f_att"][0:mid, :], att[...]))
    loads["f_ret"].wait()
    for c in second:
        c.wait()
    hidden = dot(mats["f_lat"][mid:, :], lat[...]) + (
        dot(mats["f_att"][mid:, :], att[...]) + dot(mats["f_ret"][...], recv2[...])
    )
    feed(n1, 4 * n2, hidden)
    loads["wred"].wait()
    loads["out"].wait()
    coarse = dot(merged[...], wred[...]).astype(jnp.bfloat16)
    o_ref[...] = dot(mats["out"][...], coarse).astype(jnp.bfloat16)


def per_device(lon_size, lat_size, latent, g1, wqkv, bqkv, btab, bidx, wproj, g2, wfc1, bfc1, wfc2, gm, wred):
    tr, tc, dim = latent.shape
    heads = btab.shape[1]
    mats, nw, inner, nc, sizes, starts, n1, n2, wide = plan(tr, tc)
    info = (nw, inner, nc, sizes, starts, n1, n2, wide)
    own, halo, rows = tr * tc, sum(sizes), nw * WP
    coarse = own // 4
    bf, f32 = jnp.bfloat16, jnp.float32
    any_ = pl.BlockSpec(memory_space=pl.ANY)
    vm = pl.BlockSpec(memory_space=pltpu.VMEM)
    vectors = {1, 3, 4, 5, 7, 9, 11}
    args = [latent.reshape(own, dim), g1[None], wqkv, bqkv[None], btab, bidx, wproj, g2[None], wfc1, bfc1[None], wfc2, gm[None], wred]
    args += [jnp.asarray(mats[k]) for k in MATS]
    specs = [vm if n in vectors else any_ for n in range(len(args))]
    scratch = [pltpu.VMEM(args[n].shape, bf) for n in (0, 2, 6, 8, 10, 12)]
    scratch += [pltpu.VMEM(mats[k].shape, bf) for k in MATS]
    scratch += [pltpu.VMEM((halo, dim), bf)] * 4
    scratch += [
        pltpu.VMEM((rows + 48, 3 * dim), bf),
        pltpu.VMEM((rows, dim), bf),
        pltpu.VMEM((rows, dim), bf),
        pltpu.VMEM((heads * WP, 128), f32),
        pltpu.VMEM((heads * WP, 128), f32),
        pltpu.VMEM((WP, 128), jnp.int32),
        pltpu.VMEM((256, 128), f32),
        pltpu.VMEM((4 * max(n1, n2), dim), f32),
        pltpu.VMEM((4 * max(n1, n2), wfc1.shape[1]), bf),
        pltpu.VMEM((coarse, 4 * dim), bf),
        pltpu.SemaphoreType.DMA((15,)),
        pltpu.SemaphoreType.DMA((3,)),
        pltpu.SemaphoreType.DMA((3,)),
        pltpu.SemaphoreType.DMA((3,)),
        pltpu.SemaphoreType.DMA((3,)),
    ]
    result = pl.pallas_call(
        functools.partial(kernel, info, heads, lon_size, lat_size),
        out_shape=jax.ShapeDtypeStruct((tr // 2 * wide, 2 * dim), bf),
        in_specs=specs,
        out_specs=vm,
        scratch_shapes=scratch,
        compiler_params=pltpu.CompilerParams(
            collective_id=0, has_side_effects=True, vmem_limit_bytes=56 * 1024 * 1024
        ),
        cost_estimate=pl.CostEstimate(flops=5 * 10**9, bytes_accessed=15 * 10**6, transcendentals=2 * 10**6),
    )(*args)
    return result.reshape(tr // 2, wide, 2 * dim)[:, : tc // 2]


def solution(mesh):
    in_specs = (P("lat", "lon", None),) + (P(),) * 12
    return jax.shard_map(
        functools.partial(per_device, mesh.shape["lon"], mesh.shape["lat"]),
        mesh=mesh,
        in_specs=in_specs,
        out_specs=P("lat", "lon", None),
        check_vma=False,
    )
```

time: 107 us -> 34.8 us (0.33)
  local copies, waits for them, and re-layouts: 42.2 us -> 4.54 us
  matrix products: 32.7 us -> 0 us
  Pallas kernels: 0 us -> 30 us
  waiting for transfers between devices: 12 us -> 0 us
  starting transfers between devices: 9.65 us -> 0 us
  other arithmetic: 9.63 us -> 0 us
    pallas_call x0 -> x1, Pallas kernels: none -> 30 us  [per_device(): pl.pallas_call(functools.partial(kernel, info, heads, lon_size, lat_size)...]
    dot_general x6 -> x0, matrix products: 28.3 us -> none  [the longest x1 14.7 us: per_device(): jnp.dot(inner, fc2_weight, preferred_element_type=jnp.float32)]
    ppermute x4 -> x0, waiting for transfers between devices: 12 us -> none  [shifted_2(): lax.ppermute(shard, axis, [(i, (i + by) % length) for i in range(length)])]
    another operation x3 -> x0, local copies, waits for them, and re-layouts: 10.7 us -> none  [the longest x1 6.78 us: window_attention(): qkv_windows.reshape(window_count, window_tokens, 3, head_count, head_size)]
    ppermute x4 -> x0, starting transfers between devices: 9.65 us -> none  [shifted_2(): lax.ppermute(shard, axis, [(i, (i + by) % length) for i in range(length)])]
    convert_element_type x5 -> x0, local copies, waits for them, and re-layouts: 8.55 us -> none  [the longest x3 6.2 us: layer_norm(): values = values.astype(jnp.float32)]
    reduce_sum x6 -> x0, other arithmetic: 6.82 us -> none  [the longest x3 3.86 us: layer_norm(): center = values - jnp.mean(values, axis=-1, keepdims=True)]
    transpose x2 -> x0, local copies, waits for them, and re-layouts: 5.66 us -> none  [the longest x1 4.71 us: to_windows(): return blocks.transpose(0, 2, 1, 3, 4).reshape(-1, depth * WW, channels)]
  transfers between devices with their start and end apart: 4 -> 0, of which waited for: 3 -> 0; matrix products, arithmetic and copies ran while one was open for 5% -> 0% of each run, Pallas kernels for 0% -> 0%
where the time goes in v1:
time: 34.8 us; the launch traced here: 34.5 us
  Pallas kernels  30 us (86%)
  local copies, waits for them, and re-layouts  4.54 us (13%)
    pallas_call x1, Pallas kernels, per_device(): pl.pallas_call(functools.partial(kernel, info, heads, lon_size, lat_size)...  30 us
    unnamed x2, local copies, waits for them, and re-layouts  3.25 us
    broadcast_in_dim x1, local copies, waits for them, and re-layouts, per_device(): bqkv[None]  1.28 us

profile of v1, /device:TPU:0, one launch (start us, length us, event | category | flops | bytes accessed | tf_op | source)
XLA Modules:
  0.0 34.5 jit_solution(16896849199195945430)
XLA Ops:
  0.0 1.3 %broadcast_in_dim.16.refs_3_ = f32[1,1536]{1,0:T(1,128)} reshape(f32[1536]{0:T(1024)} %param.24) | data formatting | bytes 12288 | tf_op jit(solution)/shard_map/broadcast_in_dim | solution.py:305
  1.3 1.5 %copy.22.refs_4_ = f32[253,8]{1,0:T(8,128)} copy(f32[253,8]{0,1:T(8,128)} %param.25) | data formatting | bytes 16192 | tf_op args[4]
  2.8 30.0 %shard_map.199 = bf16[192,1024]{1,0:T(8,128)(2,1)} custom-call(bf16[576,512]{1,0:T(8,128)(2,1)} %bitcast.8, f32[1,512]{1,0:T(1,128)} %bitcast.11, bf16[512,1536]{1,0:T(8,128)(2,1)} %refs_2_.1, f32[1,1536]{1,0:T(1,128)} %broadcast_in_dim.16.refs_3_, f32[253,8]{1,0:T(8,128)} %copy.22.refs_4_, s32[72,72]{1,0:T(8,128)} %refs_5_.1, bf16[512,512]{1,0:T(8,128)(2,1)} %refs_6_.1, ...), custom_call_target="tpu_custom_call" | custom-call | flops 5000000000 | bytes 15000000 | tf_op jit(solution)/shard_map/pallas_call | solution.py:328
  32.7 1.8 %copy.24 = bf16[12,12,1024]{2,1,0:T(8,128)(2,1)} copy(bf16[12,12,1024]{2,1,0:T(8,128)(2,1)} %bitcast.7) | data formatting | bytes 589824

commit v2 on v1

--- a/solution.py
+++ b/solution.py
@@ -173,10 +173,10 @@
         c.start()
 
     tab[...] = jnp.zeros_like(tab)
-    tab[0 : btab.shape[0], 0:heads] = btab[...]
+    tab[0:heads, 0 : btab.shape[1]] = btab[...]
     idx[...] = jnp.zeros_like(idx)
     idx[0:WT, 0:WT] = bidx[...]
-    lines = tab[...].T
+    lines = tab[...]
     where = idx[...]
     low, high = jnp.bitwise_and(where, 127), where >= 128
     lane = lax.broadcasted_iota(jnp.int32, (WP, 128), 1)
@@ -200,10 +200,10 @@
 
     def project(at, rows, tokens):
         normed = norm(tokens, g1[...]).astype(jnp.bfloat16)
-        qkv[at : at + rows, :] = (dot(normed, wqkv[...]) + bqkv[...]).astype(jnp.bfloat16)
+        qkv[at : at + rows, :] = (dot(normed, wqkv[...]) + bqkv[...][None, :]).astype(jnp.bfloat16)
 
     def attend(w, table):
-        at = pl.multiple_of(w * WP, 16)
+        at = w * WP
         for g in range(groups):
             col = g * 256
             q = qkv[pl.ds(at, WP), col : col + 256]
@@ -223,11 +223,8 @@
             mixed[pl.ds(at, WP), col : col + 256] = total.astype(jnp.bfloat16)
 
     def attend_range(lo, hi, table):
-        def body(w, carry):
+        for w in range(lo, hi):
             attend(w, table)
-            return carry
-
-        lax.fori_loop(lo, hi, body, 0)
 
     cut, end = inner * WP, nw * WP
     loads["p_lat"].wait()
@@ -302,7 +299,7 @@
     any_ = pl.BlockSpec(memory_space=pl.ANY)
     vm = pl.BlockSpec(memory_space=pltpu.VMEM)
     vectors = {1, 3, 4, 5, 7, 9, 11}
-    args = [latent.reshape(own, dim), g1[None], wqkv, bqkv[None], btab, bidx, wproj, g2[None], wfc1, bfc1[None], wfc2, gm[None], wred]
+    args = [latent.reshape(own, dim), g1[None], wqkv, bqkv, btab.T, bidx, wproj, g2[None], wfc1, bfc1[None], wfc2, gm[None], wred]
     args += [jnp.asarray(mats[k]) for k in MATS]
     specs = [vm if n in vectors else any_ for n in range(len(args))]
     scratch = [pltpu.VMEM(args[n].shape, bf) for n in (0, 2, 6, 8, 10, 12)]
@@ -315,7 +312,7 @@
         pltpu.VMEM((heads * WP, 128), f32),
         pltpu.VMEM((heads * WP, 128), f32),
         pltpu.VMEM((WP, 128), jnp.int32),
-        pltpu.VMEM((256, 128), f32),
+        pltpu.VMEM((heads, 256), f32),
         pltpu.VMEM((4 * max(n1, n2), dim), f32),
         pltpu.VMEM((4 * max(n1, n2), wfc1.shape[1]), bf),
         pltpu.VMEM((coarse, 4 * dim), bf),

time: 34.8 us -> 28.7 us (0.82)
  Pallas kernels: 30 us -> 26.7 us
  local copies, waits for them, and re-layouts: 4.54 us -> 1.77 us
    pallas_call x1, Pallas kernels: 30 us -> 26.7 us  [per_device(): pl.pallas_call(functools.partial(kernel, info, heads, lon_size, lat_size)...]
    unnamed x2 -> x1, local copies, waits for them, and re-layouts: 3.25 us -> 1.77 us
    broadcast_in_dim x1 -> x0, local copies, waits for them, and re-layouts: 1.28 us -> none  [per_device(): bqkv[None]]
where the time goes in v2:
time: 28.7 us; the launch traced here: 28.5 us
  Pallas kernels  26.7 us (93%)
  local copies, waits for them, and re-layouts  1.77 us (6%)
    pallas_call x1, Pallas kernels, per_device(): pl.pallas_call(functools.partial(kernel, info, heads, lon_size, lat_size)...  26.7 us
    unnamed x1, local copies, waits for them, and re-layouts  1.77 us

profile of v2, /device:TPU:0, one launch (start us, length us, event | category | flops | bytes accessed | tf_op | source)
XLA Modules:
  0.0 28.5 jit_solution(3222674709108057414)
XLA Ops:
  0.0 26.7 %shard_map.199 = bf16[192,1024]{1,0:T(8,128)(2,1)} custom-call(bf16[576,512]{1,0:T(8,128)(2,1)} %bitcast.9, f32[1,512]{1,0:T(1,128)} %bitcast.13, bf16[512,1536]{1,0:T(8,128)(2,1)} %refs_2_.1, f32[1536]{0:T(1024)} %refs_3_.1, f32[8,253]{1,0:T(8,128)} %bitcast.10, s32[72,72]{1,0:T(8,128)} %refs_5_.1, bf16[512,512]{1,0:T(8,128)(2,1)} %refs_6_.1, ...), custom_call_target="tpu_custom_call" | custom-call | flops 5000000000 | bytes 15000000 | tf_op jit(solution)/shard_map/pallas_call | solution.py:325
  26.7 1.8 %copy.23 = bf16[12,12,1024]{2,1,0:T(8,128)(2,1)} copy(bf16[12,12,1024]{2,1,0:T(8,128)(2,1)} %bitcast.8) | data formatting | bytes 589824

commit v3 on v2

--- a/solution.py
+++ b/solution.py
@@ -113,8 +113,8 @@
     o_ref = refs[21]
     (lat, wqkv, wproj, wfc1, wfc2, wred) = refs[22:28]
     mats = dict(zip(MATS, refs[28:36]))
-    (send1, recv1, send2, recv2, qkv, mixed, att, bias, last_bias, idx, tab, hid, inside, merged) = refs[36:50]
-    (load_sem, s1, r1, s2, r2) = refs[50:55]
+    (send1, recv1, send2, recv2, qkv, mixed, att, bias, last_bias, idx, tab, hid, inside, merged, local) = refs[36:51]
+    (load_sem, s1, r1, s2, r2) = refs[51:56]
     m = dict(zip(MATS, range(7, 15)))
     dim = lat.shape[1]
     head = dim // heads
@@ -236,10 +236,11 @@
     loads["wproj"].wait()
     att[0:cut, :] = dot(mixed[0:cut, :], wproj[...]).astype(jnp.bfloat16)
 
+    local[...] = dot(mats["p_lat"][cut:end, :], lat[...])
     loads["p_halo"].wait()
     for c in first:
         c.wait()
-    project(cut, end - cut, dot(mats["p_lat"][cut:end, :], lat[...]) + dot(mats["p_halo"][...], recv1[...]))
+    project(cut, end - cut, local[...] + dot(mats["p_halo"][...], recv1[...]))
     attend_range(inner, nw - nc, bias)
     attend_range(nw - nc, nw, last_bias)
     att[cut:end, :] = dot(mixed[cut:end, :], wproj[...]).astype(jnp.bfloat16)
@@ -275,13 +276,11 @@
 
     mid = 4 * n1
     feed(0, mid, dot(mats["f_lat"][0:mid, :], lat[...]) + dot(mats["f_att"][0:mid, :], att[...]))
+    local[0 : 4 * n2, :] = dot(mats["f_lat"][mid:, :], lat[...]) + dot(mats["f_att"][mid:, :], att[...])
     loads["f_ret"].wait()
     for c in second:
         c.wait()
-    hidden = dot(mats["f_lat"][mid:, :], lat[...]) + (
-        dot(mats["f_att"][mid:, :], att[...]) + dot(mats["f_ret"][...], recv2[...])
-    )
-    feed(n1, 4 * n2, hidden)
+    feed(n1, 4 * n2, local[0 : 4 * n2, :] + dot(mats["f_ret"][...], recv2[...]))
     loads["wred"].wait()
     loads["out"].wait()
     coarse = dot(merged[...], wred[...]).astype(jnp.bfloat16)
@@ -316,6 +315,7 @@
         pltpu.VMEM((4 * max(n1, n2), dim), f32),
         pltpu.VMEM((4 * max(n1, n2), wfc1.shape[1]), bf),
         pltpu.VMEM((coarse, 4 * dim), bf),
+        pltpu.VMEM((max(rows - inner * WP, 4 * n2), dim), f32),
         pltpu.SemaphoreType.DMA((15,)),
         pltpu.SemaphoreType.DMA((3,)),
         pltpu.SemaphoreType.DMA((3,)),

time: 28.7 us -> 28 us (0.976)
  Pallas kernels: 26.7 us -> 26 us
    pallas_call x1, Pallas kernels: 26.7 us -> 26 us  [per_device(): pl.pallas_call(functools.partial(kernel, info, heads, lon_size, lat_size)...]
where the time goes in v3:
time: 28 us; the launch traced here: 27.8 us
  Pallas kernels  26 us (93%)
  local copies, waits for them, and re-layouts  1.77 us (6%)
    pallas_call x1, Pallas kernels, per_device(): pl.pallas_call(functools.partial(kernel, info, heads, lon_size, lat_size)...  26 us
    unnamed x1, local copies, waits for them, and re-layouts  1.77 us

profile of v3, /device:TPU:0, one launch (start us, length us, event | category | flops | bytes accessed | tf_op | source)
XLA Modules:
  0.0 27.8 jit_solution(5045809185183596552)
XLA Ops:
  0.0 26.0 %shard_map.199 = bf16[192,1024]{1,0:T(8,128)(2,1)} custom-call(bf16[576,512]{1,0:T(8,128)(2,1)} %bitcast.9, f32[1,512]{1,0:T(1,128)} %bitcast.13, bf16[512,1536]{1,0:T(8,128)(2,1)} %refs_2_.1, f32[1536]{0:T(1024)} %refs_3_.1, f32[8,253]{1,0:T(8,128)} %bitcast.10, s32[72,72]{1,0:T(8,128)} %refs_5_.1, bf16[512,512]{1,0:T(8,128)(2,1)} %refs_6_.1, ...), custom_call_target="tpu_custom_call" | custom-call | flops 5000000000 | bytes 15000000 | tf_op jit(solution)/shard_map/pallas_call | solution.py:325
  26.0 1.8 %copy.23 = bf16[12,12,1024]{2,1,0:T(8,128)(2,1)} copy(bf16[12,12,1024]{2,1,0:T(8,128)(2,1)} %bitcast.8) | data formatting | bytes 589824
